TPU v7x, 32 devices: a whole 2x2x4 slice. The times are simulated.
32 devices in a mesh: loop: 8 (over y, x, core), grp: 4 (over z).
Axes of the slice: x: 2, y: 2, z: 4, core: 2. Of those that a mesh axis runs over, the one named last changes fastest.
Arguments:
- adjacency_tiles: bfloat16 [4096, 128, 128], P(('loop', 'grp')), may hold values from -0.046875 to 0.046875
- row_block: int32 [4096], P(('loop', 'grp')), may hold values from 0 to 7
- column_block: int32 [4096], P(('loop', 'grp')), may hold values from 0 to 3
- features: bfloat16 [4096, 256], P(('loop', 'grp')), may hold values from -6 to 6
- weight: bfloat16 [256, 256], replicated, may hold values from -0.375 to 0.375
- out_bias: float32 [256], replicated, may hold values from -3 to 3
Outputs:
- result: bfloat16 [4096, 256], P(('loop', 'grp'))
All inputs are finite; a program needn't handle non-finite values.
Results may differ from a plain program's by a relative error of at most 0.0046.
Values may be sent and summed in bfloat16 or wider, within the bound.
A program may use at most 128 MiB of HBM per device.

v0:
```python
import jax
import jax.numpy as jnp
from jax import lax
from jax.sharding import PartitionSpec as P


def on_device(adjacency_tiles, row_block, column_block, features, weight, out_bias):
    tile_size = adjacency_tiles.shape[1]
    feat_width = features.shape[1]
    loop_count = lax.axis_size("loop")
    section_rows = lax.all_gather(features, "grp", axis=0, tiled=True)
    section_blocks = section_rows.reshape(-1, tile_size, feat_width)
    picked = jnp.take(section_blocks, column_block, axis=0)
    products = jnp.einsum(
        "tij,tjf->tif", adjacency_tiles, picked, preferred_element_type=jnp.float32
    )
    partial_value = jax.ops.segment_sum(products, row_block, num_segments=loop_count)
    received = lax.all_to_all(partial_value, "loop", split_axis=0, concat_axis=0, tiled=True)
    summed = jnp.sum(received, axis=0)
    aggregate = summed.astype(jnp.bfloat16)
    mixed = jnp.dot(aggregate, weight, preferred_element_type=jnp.float32) + out_bias
    return jax.nn.relu(mixed).astype(jnp.bfloat16)


def solution(mesh):
    in_specs = (
        P(("loop", "grp"), None, None),
        P(("loop", "grp")),
        P(("loop", "grp")),
        P(("loop", "grp"), None),
        P(),
        P(),
    )
    out_specs = P(("loop", "grp"), None)
    return jax.shard_map(
        on_device, mesh=mesh, in_specs=in_specs, out_specs=out_specs, check_vma=False
    )
```

profile of v0, /device:TPU:0, one launch (start us, length us, event | category | flops | bytes accessed | tf_op | source)
XLA Modules:
  0.0 80.5 jit_solution(13343715460551516015)
XLA Ops:
  0.0 0.0 copy-start
  0.0 0.7 compare_select_fusion
  0.7 0.7 compare_and_fusion
  1.4 15.8 %all_gather.3 = bf16[512,256]{1,0:T(8,128)(2,1)S(1)} all-gather(bf16[128,256]{1,0:T(8,128)(2,1)} %param.9), channel_id=1, replica_groups=mesh['loop'=8,'grp'=4] {'grp'}, dimensions={0}, use_global_device_ids=true | all-gather | bytes 327680 | tf_op jit(solution)/shard_map/all_gather | solution.py:11
  17.2 6.5 %gather_fusion = bf16[128,128,256]{2,1,0:T(8,128)(2,1)} fusion(bf16[4,128,256]{2,1,0:T(8,128)(2,1)S(1)} %bitcast.6, s32[1024]{0:T(1024)S(1)} %pad_clamp_fusion), kind=kCustom, calls=%fused_computation | custom fusion | bytes 16777728 | tf_op jit(solution)/shard_map/jit(_take)/gather | solution.py:13
  23.7 0.0 copy-start.2
  23.7 12.8 %convolution_bitcast_fusion = f32[128,128,256]{2,1,0:T(8,128)} fusion(bf16[128,128,128]{2,1,0:T(8,128)(2,1)} %param.6, bf16[128,128,256]{2,1,0:T(8,128)(2,1)} %gather_fusion, pred[128]{0:T(512)(128)(4,1)S(1)} %compare_and_fusion), kind=kOutput, calls=%fused_computation.2 | convolution fusion | flops 1077936128 | bytes 29360256 | tf_op jit(solution)/shard_map/tij,tjf->tif/dot_general | solution.py:14
  36.5 0.1 broadcast_in_dim.19
  36.6 0.0 copy-done.2
  36.6 0.0 copy-start.1
  36.6 24.2 %scatter_fusion = f32[8,128,256]{2,1,0:T(8,128)S(1)} fusion(f32[8,128,256]{2,1,0:T(8,128)S(1)} %broadcast_in_dim.19, s32[128]{0:T(128)S(1)} %copy-done.2, f32[128,128,256]{2,1,0:T(8,128)} %convolution_bitcast_fusion), kind=kCustom, calls=%fused_computation.1 | custom fusion | flops 4194304 | bytes 50332160 | tf_op jit(solution)/shard_map/scatter-add | solution.py:17
  60.8 18.8 %all_to_all.5 = f32[8,128,256]{2,1,0:T(8,128)S(1)} all-to-all(f32[8,128,256]{2,1,0:T(8,128)S(1)} %scatter_fusion), channel_id=1, replica_groups=mesh['loop'=8,'grp'=4] {'loop'}, dimensions={0} | all-to-all | bytes 2097152 | tf_op jit(solution)/shard_map/all_to_all | solution.py:18
  79.7 0.1 reduce_sum.9
  79.7 0.0 copy-done
  79.7 0.0 copy-done.1
  79.7 0.8 fusion.4
  (1 shorter events, 0.0 us)
Async XLA Ops:
  0.0 79.7 %copy-start = (bf16[256,256]{1,0:T(8,128)(2,1)S(1)}, bf16[256,256]{1,0:T(8,128)(2,1)}, u32[]{:S(2)}) copy-start(bf16[256,256]{1,0:T(8,128)(2,1)} %param.10) | copy-start | bytes 393220
  23.7 12.9 %copy-start.2 = (s32[128]{0:T(128)S(1)}, s32[128]{0:T(128)}, u32[]{:S(2)}) copy-start(s32[128]{0:T(128)} %param.7) | copy-start | bytes 1540
  36.6 43.1 %copy-start.1 = (f32[256]{0:T(256)S(1)}, f32[256]{0:T(256)}, u32[]{:S(2)}) copy-start(f32[256]{0:T(256)} %param.11) | copy-start | bytes 3076
where the time goes:
time: 81 us; the launch traced here: 80.5 us
  blocking collectives  34.7 us (43%)
  other arithmetic  25.6 us (32%)
  matrix products  13.6 us (17%)
  local copies, waits for them, and re-layouts  6.61 us (8%)
    scatter-add x1, other arithmetic, on_device(): jax.ops.segment_sum(products, row_block, num_segments=loop_count)  24.2 us
    all_to_all x1, blocking collectives, on_device(): lax.all_to_all(partial_value, 'loop', split_axis=0, concat_axis=0, tiled=...  18.8 us
    all_gather x1, blocking collectives, on_device(): section_rows = lax.all_gather(features, 'grp', axis=0, tiled=True)  15.8 us
    dot_general x1, matrix products, on_device(): jnp.einsum('tij,tjf->tif', adjacency_tiles, picked, preferred_element_typ...  12.8 us
    gather x1, local copies, waits for them, and re-layouts, on_device(): picked = jnp.take(section_blocks, column_block, axis=0)  6.52 us

commit v1 on v0

--- a/solution.py
+++ b/solution.py
@@ -1,10 +1,17 @@
+import functools
+
 import jax
 import jax.numpy as jnp
 from jax import lax
+from jax.experimental import pallas as pl
+from jax.experimental.pallas import tpu as pltpu
 from jax.sharding import PartitionSpec as P
 
-
-def on_device(adjacency_tiles, row_block, column_block, features, weight, out_bias):
+LANES = 128
+VMEM_BYTES = 48 * 1024 * 1024
+
+
+def plain(adjacency_tiles, row_block, column_block, features, weight, out_bias):
     tile_size = adjacency_tiles.shape[1]
     feat_width = features.shape[1]
     loop_count = lax.axis_size("loop")
@@ -22,7 +29,201 @@
     return jax.nn.relu(mixed).astype(jnp.bfloat16)
 
 
+def column_sum(mask, value):
+    return jnp.sum(jnp.where(mask, value, 0), axis=0, keepdims=True)
+
+
+def sort_tables(key, count):
+    wide = jnp.broadcast_to(key, (count, count))
+    tall = wide.T
+    sub = lax.broadcasted_iota(jnp.int32, (count, count), 0)
+    lane = lax.broadcasted_iota(jnp.int32, (count, count), 1)
+    equal_before = column_sum((tall == wide) & (sub < lane), 1)
+    place = column_sum(tall < wide, 1) + equal_before
+    place_tall = jnp.broadcast_to(place, (count, count)).T
+    joins_tall = jnp.broadcast_to(equal_before, (count, count)).T
+    here = place_tall == lane
+    order = column_sum(here, sub)
+    joins = column_sum(here & (joins_tall > 0), 1)
+    last = jnp.maximum(column_sum(tall <= lane, 1) - 1, 0)
+    present = jnp.minimum(column_sum(tall == lane, 1), 1)
+    return order, joins, last, present
+
+
+def kernel(
+    loops, grps, pieces,
+    tiles_hbm, row_ref, col_ref, x_ref, w_ref, bias_ref, out_ref,
+    tiles, table_vec, table, sums, high, low, section, outgoing, incoming, own,
+    tile_sem, table_sem, xs_sem, xr_sem, ps_sem, pr_sem,
+):
+    count, side = tiles.shape[0], tiles.shape[1]
+    halves = section.shape[0]
+    width = section.shape[2]
+    my_loop, my_grp = lax.axis_index("loop"), lax.axis_index("grp")
+    step = count // pieces
+
+    loads = []
+    for i in range(pieces):
+        span = pl.ds(i * step, step)
+        loads.append(pltpu.make_async_copy(tiles_hbm.at[span], tiles.at[span], tile_sem.at[i]))
+        loads[-1].start()
+
+    barrier = pltpu.get_barrier_semaphore()
+    for d in range(1, grps):
+        pl.semaphore_signal(
+            barrier, inc=1, device_id=(my_loop, lax.rem(my_grp + d, grps)),
+            device_id_type=pl.DeviceIdType.MESH,
+        )
+    for d in range(1, loops):
+        pl.semaphore_signal(
+            barrier, inc=1, device_id=(lax.rem(my_loop + d, loops), my_grp),
+            device_id_type=pl.DeviceIdType.MESH,
+        )
+
+    rows = sort_tables(row_ref[...] * grps + col_ref[...], count)
+    for i, values in enumerate(rows):
+        table_vec[i : i + 1, :] = values
+    to_scalars = pltpu.make_async_copy(table_vec, table, table_sem)
+    to_scalars.start()
+
+    pl.semaphore_wait(barrier, grps + loops - 2)
+
+    def slot(g):
+        return pl.ds(pl.multiple_of(g * side, side), side)
+
+    def x_copy(h, target, source):
+        return pltpu.make_async_remote_copy(
+            src_ref=x_ref.at[:, pl.ds(h * width, width)],
+            dst_ref=section.at[h, slot(source)],
+            send_sem=xs_sem.at[h, target],
+            recv_sem=xr_sem.at[h, source],
+            device_id=(my_loop, target),
+            device_id_type=pl.DeviceIdType.MESH,
+        )
+
+    def p_copy(h, d, target, source):
+        return pltpu.make_async_remote_copy(
+            src_ref=outgoing.at[h, d - 1],
+            dst_ref=incoming.at[h, source],
+            send_sem=ps_sem.at[h, d - 1],
+            recv_sem=pr_sem.at[h, source],
+            device_id=(target, my_grp),
+            device_id_type=pl.DeviceIdType.MESH,
+        )
+
+    for h in range(halves):
+        for d in range(1, grps):
+            x_copy(h, lax.rem(my_grp + d, grps), my_grp).start()
+    for h in range(halves):
+        section[h, slot(my_grp), :] = x_ref[:, h * width : (h + 1) * width]
+
+    to_scalars.wait()
+    for load in loads:
+        load.wait()
+
+    def add_tile(k, total):
+        total = total * table[1, k].astype(jnp.float32) + tiles[table[0, k]].astype(jnp.float32)
+        sums[k] = total
+        return total
+
+    lax.fori_loop(0, count, add_tile, jnp.zeros((side, side), jnp.float32), unroll=4)
+
+    def split_row(r, carry):
+        for c in range(grps):
+            pair = r * grps + c
+            value = sums[table[2, pair]] * table[3, pair].astype(jnp.float32)
+            top = value.astype(jnp.bfloat16)
+            rest = (value - top.astype(jnp.float32)).astype(jnp.bfloat16)
+            high[r, :, c * side : (c + 1) * side] = top
+            low[r, :, c * side : (c + 1) * side] = rest
+        return carry
+
+    lax.fori_loop(0, loops, split_row, 0)
+
+    for h in range(halves):
+        for d in range(1, grps):
+            source = lax.rem(my_grp + d, grps)
+            x_copy(h, source, source).wait_recv()
+        block = section[h]
+        for d in range(1, loops + 1):
+            r = lax.rem(my_loop + d, loops)
+            part = jnp.dot(high[r], block, preferred_element_type=jnp.float32)
+            part = part + jnp.dot(low[r], block, preferred_element_type=jnp.float32)
+            if d < loops:
+                outgoing[h, d - 1] = part.astype(jnp.bfloat16)
+                p_copy(h, d, r, my_loop).start()
+            else:
+                own[h] = part
+
+    mixed = jnp.broadcast_to(bias_ref[...], out_ref.shape)
+    for h in range(halves):
+        total = own[h]
+        for d in range(1, loops):
+            source = lax.rem(my_loop + loops - d, loops)
+            p_copy(h, d, source, source).wait_recv()
+            total = total + incoming[h, source].astype(jnp.float32)
+        mixed = mixed + jnp.dot(
+            total.astype(jnp.bfloat16), w_ref[h * width : (h + 1) * width, :],
+            preferred_element_type=jnp.float32,
+        )
+    out_ref[...] = jnp.maximum(mixed, 0.0).astype(out_ref.dtype)
+
+    for h in range(halves):
+        for d in range(1, grps):
+            x_copy(h, lax.rem(my_grp + d, grps), my_grp).wait_send()
+        for d in range(1, loops):
+            p_copy(h, d, lax.rem(my_loop + d, loops), my_loop).wait_send()
+
+
+def on_device(loops, grps, adjacency_tiles, row_block, column_block, features, weight, out_bias):
+    count, side = adjacency_tiles.shape[0], adjacency_tiles.shape[1]
+    feat = features.shape[1]
+    halves = feat // LANES
+    pieces = 4 if count % 4 == 0 else 1
+    vmem = pl.BlockSpec(memory_space=pltpu.VMEM)
+    return pl.pallas_call(
+        functools.partial(kernel, loops, grps, pieces),
+        out_shape=jax.ShapeDtypeStruct((side, weight.shape[1]), jnp.bfloat16),
+        in_specs=[pl.BlockSpec(memory_space=pl.ANY)] + [vmem] * 5,
+        out_specs=vmem,
+        scratch_shapes=[
+            pltpu.VMEM((count, side, side), jnp.bfloat16),
+            pltpu.VMEM((8, count), jnp.int32),
+            pltpu.SMEM((8, count), jnp.int32),
+            pltpu.VMEM((count, side, side), jnp.float32),
+            pltpu.VMEM((loops, side, grps * side), jnp.bfloat16),
+            pltpu.VMEM((loops, side, grps * side), jnp.bfloat16),
+            pltpu.VMEM((halves, grps * side, LANES), jnp.bfloat16),
+            pltpu.VMEM((halves, loops, side, LANES), jnp.bfloat16),
+            pltpu.VMEM((halves, loops, side, LANES), jnp.bfloat16),
+            pltpu.VMEM((halves, side, LANES), jnp.float32),
+            pltpu.SemaphoreType.DMA((pieces,)),
+            pltpu.SemaphoreType.DMA,
+            pltpu.SemaphoreType.DMA((halves, grps)),
+            pltpu.SemaphoreType.DMA((halves, grps)),
+            pltpu.SemaphoreType.DMA((halves, loops)),
+            pltpu.SemaphoreType.DMA((halves, loops)),
+        ],
+        compiler_params=pltpu.CompilerParams(
+            collective_id=0, has_side_effects=True, vmem_limit_bytes=VMEM_BYTES
+        ),
+    )(
+        adjacency_tiles, row_block.reshape(1, count), column_block.reshape(1, count),
+        features, weight, out_bias.reshape(1, -1),
+    )
+
+
 def solution(mesh):
+    loops, grps = mesh.shape["loop"], mesh.shape["grp"]
+
+    def choose(adjacency_tiles, row_block, column_block, features, weight, out_bias):
+        count, side = adjacency_tiles.shape[0], adjacency_tiles.shape[1]
+        args = (adjacency_tiles, row_block, column_block, features, weight, out_bias)
+        fits = loops * grps <= count and count == LANES and side % LANES == 0
+        if fits and features.shape[0] == side and features.shape[1] % LANES == 0:
+            return on_device(loops, grps, *args)
+        return plain(*args)
+
     in_specs = (
         P(("loop", "grp"), None, None),
         P(("loop", "grp")),
@@ -33,5 +234,5 @@
     )
     out_specs = P(("loop", "grp"), None)
     return jax.shard_map(
-        on_device, mesh=mesh, in_specs=in_specs, out_specs=out_specs, check_vma=False
-    )
+        choose, mesh=mesh, in_specs=in_specs, out_specs=out_specs, check_vma=False
+    )

time: 81 us -> 24.6 us (0.30)
  blocking collectives: 34.7 us -> 0 us
  other arithmetic: 25.6 us -> 0 us
  Pallas kernels: 0 us -> 17.8 us
  matrix products: 13.6 us -> 0 us
    scatter-add x1 -> x0, other arithmetic: 24.2 us -> none  [on_device(): jax.ops.segment_sum(products, row_block, num_segments=loop_count)]
    all_to_all x1 -> x0, blocking collectives: 18.8 us -> none  [on_device(): lax.all_to_all(partial_value, 'loop', split_axis=0, concat_axis=0, tiled=...]
    pallas_call x0 -> x1, Pallas kernels: none -> 17.8 us  [on_device(): pl.pallas_call(functools.partial(kernel, loops, grps, pieces), out_shape=...]
    all_gather x1 -> x0, blocking collectives: 15.8 us -> none  [on_device(): section_rows = lax.all_gather(features, 'grp', axis=0, tiled=True)]
    dot_general x2 -> x0, matrix products: 13.6 us -> none  [the longest x1 12.8 us: on_device(): jnp.einsum('tij,tjf->tif', adjacency_tiles, picked, preferred_element_typ...]
    unnamed x6 -> x13, local copies, waits for them, and re-layouts: 0.01 us -> 6.55 us
    gather x1 -> x0, local copies, waits for them, and re-layouts: 6.52 us -> none  [on_device(): picked = jnp.take(section_blocks, column_block, axis=0)]
where the time goes in v1:
time: 24.6 us; the launch traced here: 24.4 us
  Pallas kernels  17.8 us (72%)
  local copies, waits for them, and re-layouts  6.55 us (27%)
    pallas_call x1, Pallas kernels, on_device(): pl.pallas_call(functools.partial(kernel, loops, grps, pieces), out_shape=...  17.8 us
    unnamed x13, local copies, waits for them, and re-layouts  6.55 us

profile of v1, /device:TPU:0, one launch (start us, length us, event | category | flops | bytes accessed | tf_op | source)
XLA Modules:
  0.0 24.4 jit_solution(11590599839319094483)
XLA Ops:
  0.0 0.0 copy-start
  0.0 2.2 %copy-done = bf16[128,128,128]{2,1,0:T(8,128)(2,1)S(1)} copy-done((bf16[128,128,128]{2,1,0:T(8,128)(2,1)S(1)}, bf16[128,128,128]{2,1,0:T(8,128)(2,1)}, u32[]{:S(2)}) %copy-start) | copy-done | bytes 4194328
  2.2 0.0 copy-start.1
  2.2 0.9 %copy-done.1 = bf16[256,256]{1,0:T(8,128)(2,1)S(1)} copy-done((bf16[256,256]{1,0:T(8,128)(2,1)S(1)}, bf16[256,256]{1,0:T(8,128)(2,1)}, u32[]{:S(2)}) %copy-start.1) | copy-done | bytes 131096
  3.1 0.0 copy-start.2
  3.1 0.8 %copy-done.2 = bf16[128,256]{1,0:T(8,128)(2,1)S(1)} copy-done((bf16[128,256]{1,0:T(8,128)(2,1)S(1)}, bf16[128,256]{1,0:T(8,128)(2,1)}, u32[]{:S(2)}) %copy-start.2) | copy-done | bytes 65560
  3.9 0.0 copy-start.3
  3.9 0.7 %copy-done.3 = f32[256]{0:T(256)S(1)} copy-done((f32[256]{0:T(256)S(1)}, f32[256]{0:T(256)}, u32[]{:S(2)}) %copy-start.3) | copy-done | bytes 1048
  4.6 0.0 copy-start.4
  4.6 0.7 %copy-done.4 = s32[128]{0:T(128)S(1)} copy-done((s32[128]{0:T(128)S(1)}, s32[128]{0:T(128)}, u32[]{:S(2)}) %copy-start.4) | copy-done | bytes 536
  5.3 0.0 copy-start.5
  5.3 0.7 %copy-done.5 = s32[128]{0:T(128)S(1)} copy-done((s32[128]{0:T(128)S(1)}, s32[128]{0:T(128)}, u32[]{:S(2)}) %copy-start.5) | copy-done | bytes 536
  5.9 17.8 %shard_map.64 = bf16[128,256]{1,0:T(8,128)(2,1)S(1)} custom-call(bf16[128,128,128]{2,1,0:T(8,128)(2,1)S(1)} %copy-done, s32[1,128]{1,0:T(1,128)S(1)} %bitcast.4, s32[1,128]{1,0:T(1,128)S(1)} %bitcast.5, bf16[128,256]{1,0:T(8,128)(2,1)S(1)} %copy-done.2, bf16[256,256]{1,0:T(8,128)(2,1)S(1)} %copy-done.1, f32[1,256]{1,0:T(1,128)S(1)} %bitcast.3), custom_call_target="tpu_custom_call" | custom-call | tf_op jit(solution)/shard_map/pallas_call | solution.py:184
  23.7 0.6 %copy.8 = bf16[128,256]{1,0:T(8,128)(2,1)} copy(bf16[128,256]{1,0:T(8,128)(2,1)S(1)} %shard_map.64) | data formatting | bytes 131072
Async XLA Ops:
  0.0 2.2 %copy-start = (bf16[128,128,128]{2,1,0:T(8,128)(2,1)S(1)}, bf16[128,128,128]{2,1,0:T(8,128)(2,1)}, u32[]{:S(2)}) copy-start(bf16[128,128,128]{2,1,0:T(8,128)(2,1)} %tiles_hbm.1) | copy-start | bytes 12582916
  2.2 0.9 %copy-start.1 = (bf16[256,256]{1,0:T(8,128)(2,1)S(1)}, bf16[256,256]{1,0:T(8,128)(2,1)}, u32[]{:S(2)}) copy-start(bf16[256,256]{1,0:T(8,128)(2,1)} %w_ref.1) | copy-start | bytes 393220
  3.1 0.8 %copy-start.2 = (bf16[128,256]{1,0:T(8,128)(2,1)S(1)}, bf16[128,256]{1,0:T(8,128)(2,1)}, u32[]{:S(2)}) copy-start(bf16[128,256]{1,0:T(8,128)(2,1)} %x_ref.1) | copy-start | bytes 196612
  3.9 0.7 %copy-start.3 = (f32[256]{0:T(256)S(1)}, f32[256]{0:T(256)}, u32[]{:S(2)}) copy-start(f32[256]{0:T(256)} %param.11) | copy-start | bytes 3076
  4.6 0.7 %copy-start.4 = (s32[128]{0:T(128)S(1)}, s32[128]{0:T(128)}, u32[]{:S(2)}) copy-start(s32[128]{0:T(128)} %param.7) | copy-start | bytes 1540
  5.3 0.7 %copy-start.5 = (s32[128]{0:T(128)S(1)}, s32[128]{0:T(128)}, u32[]{:S(2)}) copy-start(s32[128]{0:T(128)} %param.8) | copy-start | bytes 1540

commit v2 on v1

--- a/solution.py
+++ b/solution.py
@@ -8,7 +8,7 @@
 from jax.sharding import PartitionSpec as P
 
 LANES = 128
-VMEM_BYTES = 48 * 1024 * 1024
+VMEM_BYTES = 64 * 1024 * 1024
 
 
 def plain(adjacency_tiles, row_block, column_block, features, weight, out_bias):
@@ -52,9 +52,9 @@
 
 def kernel(
     loops, grps, pieces,
-    tiles_hbm, row_ref, col_ref, x_ref, w_ref, bias_ref, out_ref,
-    tiles, table_vec, table, sums, high, low, section, outgoing, incoming, own,
-    tile_sem, table_sem, xs_sem, xr_sem, ps_sem, pr_sem,
+    tiles_hbm, row_hbm, col_hbm, x_ref, w_hbm, bias_hbm, out_ref,
+    row_ref, col_ref, w_ref, bias_ref, tiles, table_vec, table, sums, high, low, section, outgoing, incoming, own,
+    in_sem, own_sem, tile_sem, table_sem, xs_sem, xr_sem, ps_sem, pr_sem,
 ):
     count, side = tiles.shape[0], tiles.shape[1]
     halves = section.shape[0]
@@ -62,6 +62,14 @@
     my_loop, my_grp = lax.axis_index("loop"), lax.axis_index("grp")
     step = count // pieces
 
+    small = [
+        pltpu.make_async_copy(source, target, in_sem.at[i])
+        for i, (source, target) in enumerate(
+            ((row_hbm, row_ref), (col_hbm, col_ref), (w_hbm, w_ref), (bias_hbm, bias_ref))
+        )
+    ]
+    small[0].start()
+    small[1].start()
     loads = []
     for i in range(pieces):
         span = pl.ds(i * step, step)
@@ -80,6 +88,8 @@
             device_id_type=pl.DeviceIdType.MESH,
         )
 
+    small[0].wait()
+    small[1].wait()
     rows = sort_tables(row_ref[...] * grps + col_ref[...], count)
     for i, values in enumerate(rows):
         table_vec[i : i + 1, :] = values
@@ -114,8 +124,14 @@
     for h in range(halves):
         for d in range(1, grps):
             x_copy(h, lax.rem(my_grp + d, grps), my_grp).start()
-    for h in range(halves):
-        section[h, slot(my_grp), :] = x_ref[:, h * width : (h + 1) * width]
+    mine = [
+        pltpu.make_async_copy(
+            x_ref.at[:, pl.ds(h * width, width)], section.at[h, slot(my_grp)], own_sem.at[h]
+        )
+        for h in range(halves)
+    ]
+    for copy in mine + small[2:]:
+        copy.start()
 
     to_scalars.wait()
     for load in loads:
@@ -144,6 +160,7 @@
         for d in range(1, grps):
             source = lax.rem(my_grp + d, grps)
             x_copy(h, source, source).wait_recv()
+        mine[h].wait()
         block = section[h]
         for d in range(1, loops + 1):
             r = lax.rem(my_loop + d, loops)
@@ -155,6 +172,8 @@
             else:
                 own[h] = part
 
+    small[2].wait()
+    small[3].wait()
     mixed = jnp.broadcast_to(bias_ref[...], out_ref.shape)
     for h in range(halves):
         total = own[h]
@@ -184,9 +203,13 @@
     return pl.pallas_call(
         functools.partial(kernel, loops, grps, pieces),
         out_shape=jax.ShapeDtypeStruct((side, weight.shape[1]), jnp.bfloat16),
-        in_specs=[pl.BlockSpec(memory_space=pl.ANY)] + [vmem] * 5,
+        in_specs=[pl.BlockSpec(memory_space=pl.ANY)] * 6,
         out_specs=vmem,
         scratch_shapes=[
+            pltpu.VMEM((1, count), jnp.int32),
+            pltpu.VMEM((1, count), jnp.int32),
+            pltpu.VMEM(weight.shape, weight.dtype),
+            pltpu.VMEM((1, weight.shape[1]), out_bias.dtype),
             pltpu.VMEM((count, side, side), jnp.bfloat16),
             pltpu.VMEM((8, count), jnp.int32),
             pltpu.SMEM((8, count), jnp.int32),
@@ -197,6 +220,8 @@
             pltpu.VMEM((halves, loops, side, LANES), jnp.bfloat16),
             pltpu.VMEM((halves, loops, side, LANES), jnp.bfloat16),
             pltpu.VMEM((halves, side, LANES), jnp.float32),
+            pltpu.SemaphoreType.DMA((4,)),
+            pltpu.SemaphoreType.DMA((halves,)),
             pltpu.SemaphoreType.DMA((pieces,)),
             pltpu.SemaphoreType.DMA,
             pltpu.SemaphoreType.DMA((halves, grps)),

time: 24.6 us -> 20 us (0.81)
  local copies, waits for them, and re-layouts: 6.55 us -> 1.47 us
  Pallas kernels: 17.8 us -> 18.4 us
    unnamed x13 -> x1, local copies, waits for them, and re-layouts: 6.55 us -> 1.47 us
    pallas_call x1, Pallas kernels: 17.8 us -> 18.4 us  [on_device(): pl.pallas_call(functools.partial(kernel, loops, grps, pieces), out_shape=...]
where the time goes in v2:
time: 20 us; the launch traced here: 19.8 us
  Pallas kernels  18.4 us (92%)
  local copies, waits for them, and re-layouts  1.47 us (7%)
    pallas_call x1, Pallas kernels, on_device(): pl.pallas_call(functools.partial(kernel, loops, grps, pieces), out_shape=...  18.4 us
    unnamed x1, local copies, waits for them, and re-layouts  1.47 us

profile of v2, /device:TPU:0, one launch (start us, length us, event | category | flops | bytes accessed | tf_op | source)
XLA Modules:
  0.0 19.8 jit_solution(4024028063540655339)
XLA Ops:
  0.0 18.4 %shard_map.64 = bf16[128,256]{1,0:T(8,128)(2,1)} custom-call(bf16[128,128,128]{2,1,0:T(8,128)(2,1)} %tiles_hbm.1, s32[1,128]{1,0:T(1,128)} %bitcast.4, s32[1,128]{1,0:T(1,128)} %bitcast.5, bf16[128,256]{1,0:T(8,128)(2,1)} %x_ref.1, bf16[256,256]{1,0:T(8,128)(2,1)} %w_hbm.1, f32[1,256]{1,0:T(1,128)} %bitcast.3), custom_call_target="tpu_custom_call" | custom-call | tf_op jit(solution)/shard_map/pallas_call | solution.py:203
  18.4 1.5 %copy.8 = bf16[128,256]{1,0:T(8,128)(2,1)} copy(bf16[128,256]{1,0:T(8,128)(2,1)} %shard_map.64) | data formatting | bytes 131072

commit v3 on v2

--- a/solution.py
+++ b/solution.py
@@ -60,6 +60,9 @@
     halves = section.shape[0]
     width = section.shape[2]
     my_loop, my_grp = lax.axis_index("loop"), lax.axis_index("grp")
+    chips = loops // 2
+    my_chip, my_core = lax.div(my_loop, 2), lax.rem(my_loop, 2)
+    sibling = 2 * my_chip + 1 - my_core
     step = count // pieces
 
     small = [
@@ -82,9 +85,12 @@
             barrier, inc=1, device_id=(my_loop, lax.rem(my_grp + d, grps)),
             device_id_type=pl.DeviceIdType.MESH,
         )
-    for d in range(1, loops):
+    pl.semaphore_signal(
+        barrier, inc=1, device_id=(sibling, my_grp), device_id_type=pl.DeviceIdType.MESH
+    )
+    for d in range(1, chips):
         pl.semaphore_signal(
-            barrier, inc=1, device_id=(lax.rem(my_loop + d, loops), my_grp),
+            barrier, inc=1, device_id=(2 * lax.rem(my_chip + d, chips) + my_core, my_grp),
             device_id_type=pl.DeviceIdType.MESH,
         )
 
@@ -96,7 +102,7 @@
     to_scalars = pltpu.make_async_copy(table_vec, table, table_sem)
     to_scalars.start()
 
-    pl.semaphore_wait(barrier, grps + loops - 2)
+    pl.semaphore_wait(barrier, grps + chips - 1)
 
     def slot(g):
         return pl.ds(pl.multiple_of(g * side, side), side)
@@ -113,13 +119,27 @@
 
     def p_copy(h, d, target, source):
         return pltpu.make_async_remote_copy(
+            src_ref=outgoing.at[h, chips + d - 1],
+            dst_ref=incoming.at[h, chips + source],
+            send_sem=ps_sem.at[h, chips + d - 1],
+            recv_sem=pr_sem.at[h, chips + source],
+            device_id=(2 * target + my_core, my_grp),
+            device_id_type=pl.DeviceIdType.MESH,
+        )
+
+    def s_copy(h, d):
+        return pltpu.make_async_remote_copy(
             src_ref=outgoing.at[h, d - 1],
-            dst_ref=incoming.at[h, source],
+            dst_ref=incoming.at[h, d - 1],
             send_sem=ps_sem.at[h, d - 1],
-            recv_sem=pr_sem.at[h, source],
-            device_id=(target, my_grp),
-            device_id_type=pl.DeviceIdType.MESH,
-        )
+            recv_sem=pr_sem.at[h, d - 1],
+            device_id=(sibling, my_grp),
+            device_id_type=pl.DeviceIdType.MESH,
+        )
+
+    def product(r, block):
+        part = jnp.dot(high[r], block, preferred_element_type=jnp.float32)
+        return part + jnp.dot(low[r], block, preferred_element_type=jnp.float32)
 
     for h in range(halves):
         for d in range(1, grps):
@@ -162,13 +182,19 @@
             x_copy(h, source, source).wait_recv()
         mine[h].wait()
         block = section[h]
-        for d in range(1, loops + 1):
-            r = lax.rem(my_loop + d, loops)
-            part = jnp.dot(high[r], block, preferred_element_type=jnp.float32)
-            part = part + jnp.dot(low[r], block, preferred_element_type=jnp.float32)
-            if d < loops:
-                outgoing[h, d - 1] = part.astype(jnp.bfloat16)
-                p_copy(h, d, r, my_loop).start()
+        for d in range(1, chips + 1):
+            chip = lax.rem(my_chip + d, chips)
+            part = product(2 * chip + 1 - my_core, block)
+            outgoing[h, d - 1] = part.astype(jnp.bfloat16)
+            s_copy(h, d).start()
+        for d in range(1, chips + 1):
+            chip = lax.rem(my_chip + d, chips)
+            part = product(2 * chip + my_core, block)
+            s_copy(h, d).wait_recv()
+            part = part + incoming[h, d - 1].astype(jnp.float32)
+            if d < chips:
+                outgoing[h, chips + d - 1] = part.astype(jnp.bfloat16)
+                p_copy(h, d, chip, my_chip).start()
             else:
                 own[h] = part
 
@@ -177,10 +203,10 @@
     mixed = jnp.broadcast_to(bias_ref[...], out_ref.shape)
     for h in range(halves):
         total = own[h]
-        for d in range(1, loops):
-            source = lax.rem(my_loop + loops - d, loops)
+        for d in range(1, chips):
+            source = lax.rem(my_chip + chips - d, chips)
             p_copy(h, d, source, source).wait_recv()
-            total = total + incoming[h, source].astype(jnp.float32)
+            total = total + incoming[h, chips + source].astype(jnp.float32)
         mixed = mixed + jnp.dot(
             total.astype(jnp.bfloat16), w_ref[h * width : (h + 1) * width, :],
             preferred_element_type=jnp.float32,
@@ -190,8 +216,10 @@
     for h in range(halves):
         for d in range(1, grps):
             x_copy(h, lax.rem(my_grp + d, grps), my_grp).wait_send()
-        for d in range(1, loops):
-            p_copy(h, d, lax.rem(my_loop + d, loops), my_loop).wait_send()
+        for d in range(1, chips + 1):
+            s_copy(h, d).wait_send()
+        for d in range(1, chips):
+            p_copy(h, d, lax.rem(my_chip + d, chips), my_chip).wait_send()
 
 
 def on_device(loops, grps, adjacency_tiles, row_block, column_block, features, weight, out_bias):
@@ -244,7 +272,7 @@
     def choose(adjacency_tiles, row_block, column_block, features, weight, out_bias):
         count, side = adjacency_tiles.shape[0], adjacency_tiles.shape[1]
         args = (adjacency_tiles, row_block, column_block, features, weight, out_bias)
-        fits = loops * grps <= count and count == LANES and side % LANES == 0
+        fits = loops % 2 == 0 and loops * grps <= count and count == LANES and side % LANES == 0
         if fits and features.shape[0] == side and features.shape[1] % LANES == 0:
             return on_device(loops, grps, *args)
         return plain(*args)

time: 20 us -> 21 us (1.050)
  Pallas kernels: 18.4 us -> 19.4 us
    pallas_call x1, Pallas kernels: 18.4 us -> 19.4 us  [on_device(): pl.pallas_call(functools.partial(kernel, loops, grps, pieces), out_shape=...]
where the time goes in v3:
time: 21 us; the launch traced here: 20.9 us
  Pallas kernels  19.4 us (92%)
  local copies, waits for them, and re-layouts  1.47 us (7%)
    pallas_call x1, Pallas kernels, on_device(): pl.pallas_call(functools.partial(kernel, loops, grps, pieces), out_shape=...  19.4 us
    unnamed x1, local copies, waits for them, and re-layouts  1.47 us

profile of v3, /device:TPU:0, one launch (start us, length us, event | category | flops | bytes accessed | tf_op | source)
XLA Modules:
  0.0 20.9 jit_solution(13926240016824450629)
XLA Ops:
  0.0 19.4 %shard_map.64 = bf16[128,256]{1,0:T(8,128)(2,1)} custom-call(bf16[128,128,128]{2,1,0:T(8,128)(2,1)} %tiles_hbm.1, s32[1,128]{1,0:T(1,128)} %bitcast.4, s32[1,128]{1,0:T(1,128)} %bitcast.5, bf16[128,256]{1,0:T(8,128)(2,1)} %x_ref.1, bf16[256,256]{1,0:T(8,128)(2,1)} %w_hbm.1, f32[1,256]{1,0:T(1,128)} %bitcast.3), custom_call_target="tpu_custom_call" | custom-call | tf_op jit(solution)/shard_map/pallas_call | solution.py:231
  19.4 1.5 %copy.8 = bf16[128,256]{1,0:T(8,128)(2,1)} copy(bf16[128,256]{1,0:T(8,128)(2,1)} %shard_map.64) | data formatting | bytes 131072

commit v4 on v2

--- a/solution.py
+++ b/solution.py
@@ -197,7 +197,8 @@
 def on_device(loops, grps, adjacency_tiles, row_block, column_block, features, weight, out_bias):
     count, side = adjacency_tiles.shape[0], adjacency_tiles.shape[1]
     feat = features.shape[1]
-    halves = feat // LANES
+    halves = 1
+    width = feat // halves
     pieces = 4 if count % 4 == 0 else 1
     vmem = pl.BlockSpec(memory_space=pltpu.VMEM)
     return pl.pallas_call(
@@ -216,10 +217,10 @@
             pltpu.VMEM((count, side, side), jnp.float32),
             pltpu.VMEM((loops, side, grps * side), jnp.bfloat16),
             pltpu.VMEM((loops, side, grps * side), jnp.bfloat16),
-            pltpu.VMEM((halves, grps * side, LANES), jnp.bfloat16),
-            pltpu.VMEM((halves, loops, side, LANES), jnp.bfloat16),
-            pltpu.VMEM((halves, loops, side, LANES), jnp.bfloat16),
-            pltpu.VMEM((halves, side, LANES), jnp.float32),
+            pltpu.VMEM((halves, grps * side, width), jnp.bfloat16),
+            pltpu.VMEM((halves, loops, side, width), jnp.bfloat16),
+            pltpu.VMEM((halves, loops, side, width), jnp.bfloat16),
+            pltpu.VMEM((halves, side, width), jnp.float32),
             pltpu.SemaphoreType.DMA((4,)),
             pltpu.SemaphoreType.DMA((halves,)),
             pltpu.SemaphoreType.DMA((pieces,)),

time: 20 us -> 20.8 us (1.040)
  Pallas kernels: 18.4 us -> 19.1 us
    pallas_call x1, Pallas kernels: 18.4 us -> 19.1 us  [on_device(): pl.pallas_call(functools.partial(kernel, loops, grps, pieces), out_shape=...]
where the time goes in v4:
time: 20.8 us; the launch traced here: 20.6 us
  Pallas kernels  19.1 us (92%)
  local copies, waits for them, and re-layouts  1.47 us (7%)
    pallas_call x1, Pallas kernels, on_device(): pl.pallas_call(functools.partial(kernel, loops, grps, pieces), out_shape=...  19.1 us
    unnamed x1, local copies, waits for them, and re-layouts  1.47 us

profile of v4, /device:TPU:0, one launch (start us, length us, event | category | flops | bytes accessed | tf_op | source)
XLA Modules:
  0.0 20.6 jit_solution(136696899278921656)
XLA Ops:
  0.0 19.1 %shard_map.64 = bf16[128,256]{1,0:T(8,128)(2,1)} custom-call(bf16[128,128,128]{2,1,0:T(8,128)(2,1)} %tiles_hbm.1, s32[1,128]{1,0:T(1,128)} %bitcast.4, s32[1,128]{1,0:T(1,128)} %bitcast.5, bf16[128,256]{1,0:T(8,128)(2,1)} %x_ref.1, bf16[256,256]{1,0:T(8,128)(2,1)} %w_hbm.1, f32[1,256]{1,0:T(1,128)} %bitcast.3), custom_call_target="tpu_custom_call" | custom-call | tf_op jit(solution)/shard_map/pallas_call | solution.py:204
  19.1 1.5 %copy.8 = bf16[128,256]{1,0:T(8,128)(2,1)} copy(bf16[128,256]{1,0:T(8,128)(2,1)} %shard_map.64) | data formatting | bytes 131072

commit v5 on v2

--- a/solution.py
+++ b/solution.py
@@ -185,7 +185,7 @@
             total.astype(jnp.bfloat16), w_ref[h * width : (h + 1) * width, :],
             preferred_element_type=jnp.float32,
         )
-    out_ref[...] = jnp.maximum(mixed, 0.0).astype(out_ref.dtype)
+    out_ref[...] = mixed.astype(out_ref.dtype)
 
     for h in range(halves):
         for d in range(1, grps):
@@ -200,7 +200,7 @@
     halves = feat // LANES
     pieces = 4 if count % 4 == 0 else 1
     vmem = pl.BlockSpec(memory_space=pltpu.VMEM)
-    return pl.pallas_call(
+    mixed = pl.pallas_call(
         functools.partial(kernel, loops, grps, pieces),
         out_shape=jax.ShapeDtypeStruct((side, weight.shape[1]), jnp.bfloat16),
         in_specs=[pl.BlockSpec(memory_space=pl.ANY)] * 6,
@@ -236,6 +236,7 @@
         adjacency_tiles, row_block.reshape(1, count), column_block.reshape(1, count),
         features, weight, out_bias.reshape(1, -1),
     )
+    return jax.nn.relu(mixed)
 
 
 def solution(mesh):

time: 20 us -> 20 us (level)
  other arithmetic: 0 us -> 1.47 us
  local copies, waits for them, and re-layouts: 1.47 us -> 0 us
    max x0 -> x1, other arithmetic: none -> 1.47 us  [on_device(): return jax.nn.relu(mixed)]
    unnamed x1 -> x0, local copies, waits for them, and re-layouts: 1.47 us -> none
where the time goes in v5:
time: 20 us; the launch traced here: 19.8 us
  Pallas kernels  18.4 us (92%)
  other arithmetic  1.47 us (7%)
    pallas_call x1, Pallas kernels, on_device(): pl.pallas_call(functools.partial(kernel, loops, grps, pieces), out_shape=...  18.4 us
    max x1, other arithmetic, on_device(): return jax.nn.relu(mixed)  1.47 us

profile of v5, /device:TPU:0, one launch (start us, length us, event | category | flops | bytes accessed | tf_op | source)
XLA Modules:
  0.0 19.8 jit_solution(11783636510697595536)
XLA Ops:
  0.0 18.4 %shard_map.64 = bf16[128,256]{1,0:T(8,128)(2,1)} custom-call(bf16[128,128,128]{2,1,0:T(8,128)(2,1)} %tiles_hbm.1, s32[1,128]{1,0:T(1,128)} %bitcast.4, s32[1,128]{1,0:T(1,128)} %bitcast.5, bf16[128,256]{1,0:T(8,128)(2,1)} %x_ref.1, bf16[256,256]{1,0:T(8,128)(2,1)} %w_hbm.1, f32[1,256]{1,0:T(1,128)} %bitcast.3), custom_call_target="tpu_custom_call" | custom-call | tf_op jit(solution)/shard_map/pallas_call | solution.py:203
  18.4 1.5 %broadcast_maximum_fusion = bf16[128,256]{1,0:T(8,128)(2,1)} fusion(bf16[128,256]{1,0:T(8,128)(2,1)} %shard_map.64), kind=kLoop, calls=%fused_computation | loop fusion | flops 32768 | bytes 131072 | tf_op jit(solution)/shard_map/jit(relu)/max | solution.py:239
